TPU v7x, 32 devices: a whole 2x2x4 slice. The times are simulated.
32 devices in a mesh: rows: 8 (over z, x), cols: 4 (over y, core).
Axes of the slice: x: 2, y: 2, z: 4, core: 2. Of those that a mesh axis runs over, the one named last changes fastest.
Arguments:
- h_blocks: float32 [64, 48, 64, 64], P('rows', 'cols'), may hold values from -0.109375 to 0.109375
- p_blocks: float32 [64, 48, 64, 64], P('rows', 'cols'), may hold values from -0.109375 to 0.109375
- h_fetch: int32 [8, 8, 2], P('rows'), may hold values from 0 to 7
- p_fetch: int32 [8, 8, 2], P('rows'), may hold values from 0 to 7
- h_slot: int32 [64, 48], P('rows'), may hold values from 0 to 15
- p_slot: int32 [64, 48], P('rows'), may hold values from 0 to 15
- p_panel: float32 [4096, 1024], P('rows', 'cols'), may hold values from -6 to 6
Outputs:
- w_panel: float32 [4096, 1024], P('rows', 'cols')
Inputs may be any that keep to these rules, and one draw needn't show every extreme that they name: `p_fetch`: local block rows of the owner. `h_slot`: slot 2 * o + c names entry c of the owner o's fetch list. `p_slot`: slot 2 * o + c names entry c of the owner o's fetch list.
All inputs are finite; a program needn't handle non-finite values.
Results may differ from a plain program's by a relative error of at most 0.000098.
Values sent between devices are 32-bit elements; how exact they have to be, the bound alone decides.
A program may use at most 128 MiB of HBM per device.

v0:
```python
import jax
import jax.numpy as jnp
from jax import lax
from jax.sharding import PartitionSpec as P

highest = lax.Precision.HIGHEST


def multiply(block_list, fetch_lists, slot_lists, panel_part):
    own_rows = block_list.shape[0]
    block_size = block_list.shape[2]
    columns = panel_part.shape[1]
    wanted = lax.all_to_all(fetch_lists[0], "rows", split_axis=0, concat_axis=0, tiled=True)
    stacked = panel_part.reshape(own_rows, block_size, columns)
    packed = jnp.take(stacked, wanted, axis=0)
    arrived = lax.all_to_all(packed, "rows", split_axis=0, concat_axis=0, tiled=True)
    flattened = arrived.reshape(-1, block_size, columns)
    chosen = jnp.take(flattened, slot_lists, axis=0)
    result = jnp.einsum("ijab,ijbc->iac", block_list, chosen, precision=highest)
    return result.reshape(own_rows * block_size, columns)


def body(h_blocks, p_blocks, h_fetch, p_fetch, h_slot, p_slot, p_panel):
    gathered = (
        lax.all_gather(h_blocks, "cols", axis=1, tiled=True),
        lax.all_gather(p_blocks, "cols", axis=1, tiled=True),
    )
    middle = multiply(gathered[0], h_fetch, h_slot, p_panel)
    return multiply(gathered[1], p_fetch, p_slot, middle)


def solution(mesh):
    in_specs = (
        P("rows", "cols", None, None),
        P("rows", "cols", None, None),
        P("rows", None, None),
        P("rows", None, None),
        P("rows", None),
        P("rows", None),
        P("rows", "cols"),
    )
    out_specs = P("rows", "cols")
    return jax.shard_map(body, mesh=mesh, in_specs=in_specs, out_specs=out_specs, check_vma=False)
```

profile of v0, /device:TPU:0, one launch (start us, length us, event | category | flops | bytes accessed | tf_op | source)
XLA Modules:
  0.0 205.7 jit_solution(2170772187894085556)
XLA Ops:
  6.5 0.0 copy-start
  6.5 0.0 all-gather.3.cloned.1.call-start
  6.5 0.7 all-gather.3.cloned.1.call-update
  7.3 0.0 all-gather.5.cloned.1.call-start
  7.3 0.7 all-gather.5.cloned.1.call-update
  8.0 1.3 copy.19
  9.4 7.3 %all-to-all-start = ((s32[8,1,2]{2,1,0:T(1,128)}), s32[8,1,2]{2,1,0:T(1,128)S(1)}, u32[]{:S(2)}, u32[]{:S(2)}) async-start(s32[8,1,2]{2,1,0:T(1,128)} %copy.19), calls=%async_computation | async-start | bytes 8192 | tf_op jit(solution)/shard_map/all_to_all | solution.py:13
  16.6 1.3 copy.16
  18.0 5.0 %all-to-all-done = s32[8,1,2]{2,1,0:T(1,128)S(1)} async-done(((s32[8,1,2]{2,1,0:T(1,128)}), s32[8,1,2]{2,1,0:T(1,128)S(1)}, u32[]{:S(2)}, u32[]{:S(2)}) %all-to-all-start) | async-done | bytes 96 | tf_op jit(solution)/shard_map/all_to_all | solution.py:13
  23.0 3.3 %all-to-all-start.2 = ((s32[8,1,2]{2,1,0:T(1,128)}), s32[8,1,2]{2,1,0:T(1,128)S(1)}, u32[]{:S(2)}, u32[]{:S(2)}) async-start(s32[8,1,2]{2,1,0:T(1,128)} %copy.16), calls=%async_computation.2 | async-start | bytes 8192 | tf_op jit(solution)/shard_map/all_to_all | solution.py:13
  26.3 0.1 copy.20
  26.4 0.1 copy.22
  26.4 0.1 reshape.72
  26.5 0.1 copy.21
  26.6 0.0 copy-done
  26.6 0.6 gather_fusion
  27.3 1.1 broadcast_select_fusion.1
  28.4 4.3 %all-to-all-done.2 = s32[8,1,2]{2,1,0:T(1,128)S(1)} async-done(((s32[8,1,2]{2,1,0:T(1,128)}), s32[8,1,2]{2,1,0:T(1,128)S(1)}, u32[]{:S(2)}, u32[]{:S(2)}) %all-to-all-start.2) | async-done | bytes 96 | tf_op jit(solution)/shard_map/all_to_all | solution.py:13
  32.7 3.6 %all-to-all-start.1 = ((f32[8,2,64,256]{3,2,1,0:T(8,128)}), f32[8,2,64,256]{3,2,1,0:T(8,128)S(1)}, u32[]{:S(2)}, u32[]{:S(2)}) async-start(f32[8,2,64,256]{3,2,1,0:T(8,128)} %broadcast_select_fusion.1), calls=%async_computation.1 | async-start | bytes 2097152 | tf_op jit(solution)/shard_map/all_to_all | solution.py:16
  36.2 0.7 compare_select_fusion.1
  36.9 0.1 reshape.76
  37.0 0.7 compare_and_fusion.1
  37.7 0.1 copy.17
  37.8 0.1 copy.23
  37.9 0.1 reshape.80
  38.0 0.1 copy.18
  38.1 21.7 %all-to-all-done.1 = f32[8,2,64,256]{3,2,1,0:T(8,128)S(1)} async-done(((f32[8,2,64,256]{3,2,1,0:T(8,128)}), f32[8,2,64,256]{3,2,1,0:T(8,128)S(1)}, u32[]{:S(2)}, u32[]{:S(2)}) %all-to-all-start.1) | async-done | bytes 1048608 | tf_op jit(solution)/shard_map/all_to_all | solution.py:16
  59.8 10.0 %gather_fusion.1 = f32[384,64,256]{2,1,0:T(8,128)} fusion(f32[16,64,256]{2,1,0:T(8,128)S(1)} %bitcast.31, s32[1024]{0:T(1024)S(1)} %pad_clamp_fusion.2), kind=kCustom, calls=%fused_computation.1.clone | custom fusion | bytes 50333184 | tf_op jit(solution)/shard_map/jit(_take)/gather | solution.py:18
  69.9 23.9 %all-gather.3.cloned.1.call-done = f32[8,48,64,64]{3,2,1,0:T(8,128)} async-done(((f32[8,12,64,64]{3,2,1,0:T(8,128)}), f32[8,48,64,64]{3,2,1,0:T(8,128)}) %all-gather.3.cloned.1.call-update) | async-done | bytes 6291472 | tf_op jit(solution)/shard_map/all_gather | solution.py:25
  93.8 0.0 copy-start.2
  93.8 22.3 %fusion.8 = f32[8,64,256]{2,1,0:T(8,128)S(1)} fusion(f32[8,48,64,64]{3,2,1,0:T(8,128)} %all-gather.3.cloned.1.call-done, f32[8,48,64,256]{3,2,1,0:T(8,128)} %bitcast.33, pred[8,48]{1,0:T(8,128)(4,1)S(1)} %compare_and_fusion.1), kind=kOutput, calls=%fused_computation.12 | convolution fusion | flops 4838129664 | bytes 31981952 | tf_op jit(solution)/shard_map/ijab,ijbc->iac/dot_general | solution.py:19
  116.1 0.6 gather_fusion.2
  116.7 1.1 broadcast_select_fusion
  117.9 5.5 %all-to-all-start.3 = ((f32[8,2,64,256]{3,2,1,0:T(8,128)}), f32[8,2,64,256]{3,2,1,0:T(8,128)S(1)}, u32[]{:S(2)}, u32[]{:S(2)}) async-start(f32[8,2,64,256]{3,2,1,0:T(8,128)} %broadcast_select_fusion), calls=%async_computation.3 | async-start | bytes 2097152 | tf_op jit(solution)/shard_map/all_to_all | solution.py:16
  123.4 0.0 copy-done.2
  123.4 0.1 reshape.84
  123.5 26.1 %all-to-all-done.3 = f32[8,2,64,256]{3,2,1,0:T(8,128)S(1)} async-done(((f32[8,2,64,256]{3,2,1,0:T(8,128)}), f32[8,2,64,256]{3,2,1,0:T(8,128)S(1)}, u32[]{:S(2)}, u32[]{:S(2)}) %all-to-all-start.3) | async-done | bytes 1048608 | tf_op jit(solution)/shard_map/all_to_all | solution.py:16
  149.6 0.0 copy-start.1
  149.6 9.9 %gather_fusion.3 = f32[384,64,256]{2,1,0:T(8,128)} fusion(f32[16,64,256]{2,1,0:T(8,128)S(1)} %bitcast.32, s32[1024]{0:T(1024)S(1)} %pad_clamp_fusion), kind=kCustom, calls=%fused_computation.3.clone | custom fusion | bytes 50333184 | tf_op jit(solution)/shard_map/jit(_take)/gather | solution.py:18
  159.5 17.9 %all-gather.5.cloned.1.call-done = f32[8,48,64,64]{3,2,1,0:T(8,128)} async-done(((f32[8,12,64,64]{3,2,1,0:T(8,128)}), f32[8,48,64,64]{3,2,1,0:T(8,128)}) %all-gather.5.cloned.1.call-update) | async-done | bytes 6291472 | tf_op jit(solution)/shard_map/all_gather | solution.py:26
  177.5 21.4 %fusion = f32[8,256,64,1]{1,2,3,0:T(8,128)} fusion(f32[8,48,64,64]{3,2,1,0:T(8,128)} %all-gather.5.cloned.1.call-done, f32[8,48,64,256]{3,2,1,0:T(8,128)} %bitcast.34, pred[8,48]{1,0:T(8,128)(4,1)S(1)} %compare_and_fusion), kind=kOutput, calls=%fused_computation.4 | convolution fusion | flops 4838129664 | bytes 31981952 | tf_op jit(solution)/shard_map/ijab,ijbc->iac/dot_general | solution.py:19
  198.9 0.0 copy-done.1
  (10 shorter events, 0.1 us)
Async XLA Ops:
  6.5 20.1 %copy-start = (f32[512,256]{1,0:T(8,128)S(1)}, f32[512,256]{1,0:T(8,128)}, u32[]{:S(2)}) copy-start(f32[512,256]{1,0:T(8,128)} %param.17) | copy-start | bytes 1572868
  6.5 87.2 %all-gather.3.cloned.1.call-start = ((), (), s32[]{:S(2)}) async-start(), calls=%async_computation.4 | async-start | bytes 15728640 | tf_op jit(solution)/shard_map/all_gather | solution.py:25
  7.3 170.2 %all-gather.5.cloned.1.call-start = ((), (), s32[]{:S(2)}) async-start(), calls=%async_computation.5 | async-start | bytes 15728640 | tf_op jit(solution)/shard_map/all_gather | solution.py:26
  9.4 13.6 %all-to-all-start = ((s32[8,1,2]{2,1,0:T(1,128)}), s32[8,1,2]{2,1,0:T(1,128)S(1)}, u32[]{:S(2)}, u32[]{:S(2)}) async-start(s32[8,1,2]{2,1,0:T(1,128)} %copy.19), calls=%async_computation | async-start | bytes 8192 | tf_op jit(solution)/shard_map/all_to_all | solution.py:13
  23.0 9.7 %all-to-all-start.2 = ((s32[8,1,2]{2,1,0:T(1,128)}), s32[8,1,2]{2,1,0:T(1,128)S(1)}, u32[]{:S(2)}, u32[]{:S(2)}) async-start(s32[8,1,2]{2,1,0:T(1,128)} %copy.16), calls=%async_computation.2 | async-start | bytes 8192 | tf_op jit(solution)/shard_map/all_to_all | solution.py:13
  32.7 27.1 %all-to-all-start.1 = ((f32[8,2,64,256]{3,2,1,0:T(8,128)}), f32[8,2,64,256]{3,2,1,0:T(8,128)S(1)}, u32[]{:S(2)}, u32[]{:S(2)}) async-start(f32[8,2,64,256]{3,2,1,0:T(8,128)} %broadcast_select_fusion.1), calls=%async_computation.1 | async-start | bytes 2097152 | tf_op jit(solution)/shard_map/all_to_all | solution.py:16
  93.8 29.6 %copy-start.2 = (s32[8,48]{1,0:T(8,128)S(1)}, s32[8,48]{1,0:T(8,128)}, u32[]{:S(2)}) copy-start(s32[8,48]{1,0:T(8,128)} %param.16) | copy-start | bytes 4612
  117.9 31.8 %all-to-all-start.3 = ((f32[8,2,64,256]{3,2,1,0:T(8,128)}), f32[8,2,64,256]{3,2,1,0:T(8,128)S(1)}, u32[]{:S(2)}, u32[]{:S(2)}) async-start(f32[8,2,64,256]{3,2,1,0:T(8,128)} %broadcast_select_fusion), calls=%async_computation.3 | async-start | bytes 2097152 | tf_op jit(solution)/shard_map/all_to_all | solution.py:16
  149.6 49.3 %copy-start.1 = (f32[512,256]{1,0:T(8,128)S(1)}, f32[512,256]{1,0:T(8,128)}, u32[]{:S(2)}) copy-start(f32[512,256]{1,0:T(8,128)} %param.17) | copy-start | bytes 1572868
Sparse Core Ops, SparseCore 0:
  8.9 84.7 all-gather.2
  95.3 82.0 all-gather.4
where the time goes:
time: 206 us
  waiting for transfers between devices  100 us (49%)
  matrix products  43.8 us (21%)
  local copies, waits for them, and re-layouts  24.8 us (12%)
  starting transfers between devices  19.7 us (10%)
  between operations  13.5 us (7%)
  other arithmetic  3.68 us (2%)
    all_to_all x2, waiting for transfers between devices, multiply(): lax.all_to_all(packed, 'rows', split_axis=0, concat_axis=0, tiled=True)  47.8 us
    dot_general x2, matrix products, multiply(): result = jnp.einsum('ijab,ijbc->iac', block_list, chosen, precision=highest)  43.8 us
    all_gather x1, waiting for transfers between devices, body(): lax.all_gather(h_blocks, 'cols', axis=1, tiled=True)  23.9 us
    gather x2, local copies, waits for them, and re-layouts, multiply(): chosen = jnp.take(flattened, slot_lists, axis=0)  20 us
    all_gather x1, waiting for transfers between devices, body(): lax.all_gather(p_blocks, 'cols', axis=1, tiled=True)  17.9 us
    all_to_all x2, starting transfers between devices, multiply(): lax.all_to_all(fetch_lists[0], 'rows', split_axis=0, concat_axis=0, tiled...  10.5 us
    all_to_all x2, waiting for transfers between devices, multiply(): lax.all_to_all(fetch_lists[0], 'rows', split_axis=0, concat_axis=0, tiled...  9.33 us
    all_to_all x2, starting transfers between devices, multiply(): lax.all_to_all(packed, 'rows', split_axis=0, concat_axis=0, tiled=True)  9.1 us
  transfers between devices with their start and end apart: 6, of which 6 were waited for; matrix products, arithmetic and copies ran while one was open for 25% of the time, Pallas kernels for 0%

commit v1 on v0

v1 whole, which is shorter than its diff:
```python
import functools

import jax
import jax.numpy as jnp
from jax import lax
from jax.experimental import pallas as pl
from jax.experimental.pallas import tpu as pltpu
from jax.sharding import PartitionSpec as P

highest = lax.Precision.HIGHEST
MESH = pl.DeviceIdType.MESH
LANES = 128


def take_kernel(indices, slab, out):
    out[...] = slab[...]


def take_slabs(slabs, indices):
    _, b, columns = slabs.shape
    slab = (1, b, columns)
    taken = pl.pallas_call(
        take_kernel,
        out_shape=jax.ShapeDtypeStruct((indices.size, b, columns), slabs.dtype),
        grid_spec=pltpu.PrefetchScalarGridSpec(
            num_scalar_prefetch=1,
            grid=(indices.size,),
            in_specs=[pl.BlockSpec(slab, lambda i, wanted: (wanted[i], 0, 0))],
            out_specs=pl.BlockSpec(slab, lambda i, wanted: (i, 0, 0)),
        ),
        name="take_slabs",
    )(indices.reshape(-1), slabs)
    return taken.reshape(*indices.shape, b, columns)


def multiply(block_list, fetch_lists, slot_lists, panel_part):
    own_rows = block_list.shape[0]
    block_size = block_list.shape[2]
    columns = panel_part.shape[1]
    wanted = lax.all_to_all(fetch_lists[0], "rows", split_axis=0, concat_axis=0, tiled=True)
    stacked = panel_part.reshape(own_rows, block_size, columns)
    packed = take_slabs(stacked, wanted)
    arrived = lax.all_to_all(packed, "rows", split_axis=0, concat_axis=0, tiled=True)
    flattened = arrived.reshape(-1, block_size, columns)
    chosen = take_slabs(flattened, slot_lists)
    result = jnp.einsum("ijab,ijbc->iac", block_list, chosen, precision=highest)
    return result.reshape(own_rows * block_size, columns)


def list_body(h_blocks, p_blocks, h_fetch, p_fetch, h_slot, p_slot, p_panel):
    gathered = (
        lax.all_gather(h_blocks, "cols", axis=1, tiled=True),
        lax.all_gather(p_blocks, "cols", axis=1, tiled=True),
    )
    middle = multiply(gathered[0], h_fetch, h_slot, p_panel)
    return multiply(gathered[1], p_fetch, p_slot, middle)


def merge_kernel(cap, h_slot, p_slot, h_blocks, p_blocks, h_out, p_out):
    i = pl.program_id(0)
    n_local, b = h_blocks.shape[1], h_blocks.shape[2]
    first = lax.axis_index("cols") * n_local
    lane_part = lax.broadcasted_iota(jnp.int32, (b, cap * b), 1) // b
    for slots, blocks, out in ((h_slot, h_blocks, h_out), (p_slot, p_blocks, p_out)):
        out[...] = jnp.zeros_like(out)
        for j in range(n_local):
            slot = slots[i, first + j]
            owner, part = slot // cap, slot % cap
            block = blocks[0, j]
            wide = jnp.concatenate([block] * cap, axis=1)
            out[owner] += jnp.where(lane_part == part, wide, 0.0)


def merge(h_slot, p_slot, h_blocks, p_blocks, n_rows, cap):
    own_rows, n_local, b, _ = h_blocks.shape
    blocks = pl.BlockSpec((1, n_local, b, b), lambda i, *_: (i, 0, 0, 0))
    merged = pl.BlockSpec((n_rows, b, cap * b), lambda i, *_: (0, i, 0))
    shape = jax.ShapeDtypeStruct((n_rows, own_rows * b, cap * b), jnp.float32)
    return pl.pallas_call(
        functools.partial(merge_kernel, cap),
        out_shape=(shape, shape),
        grid_spec=pltpu.PrefetchScalarGridSpec(
            num_scalar_prefetch=2, grid=(own_rows,), in_specs=[blocks, blocks], out_specs=[merged, merged]
        ),
        name="merge",
    )(h_slot, p_slot, h_blocks, p_blocks)


def split(x):
    high = x.astype(jnp.bfloat16)
    return high, (x - high.astype(jnp.float32)).astype(jnp.bfloat16)


def product_kernel(
    n_rows, n_cols, cap, b,
    dh, dp, fetch, panel, out,
    lists, wanted, rs_buf, y_send, y_recv, total, from_sib, d_high, d_low,
    packed, slots, b_both, x_buf,
    list_s, list_r, list_l, rs_s, rs_r, y_s, y_r, ag_s, ag_r, slot_s, slot_r,
):
    me, c = lax.axis_index("rows"), lax.axis_index("cols")
    core = lax.rem(c, 2)
    sibling = c + 1 - 2 * core
    across = lax.rem(c + 2, n_cols)
    per_half = n_rows // 2
    mine, theirs = core * per_half, (1 - core) * per_half
    halves = panel.shape[2] // LANES
    depth = cap * b
    rows_all = panel.shape[0] * b

    def right(k):
        return lax.rem(me + k, n_rows)

    def left(k):
        return lax.rem(me + n_rows - k, n_rows)

    barrier = pltpu.get_barrier_semaphore()
    for k in range(1, n_rows):
        pl.semaphore_signal(barrier, inc=1, device_id={"rows": right(k)}, device_id_type=MESH)
    for other in (sibling, across):
        pl.semaphore_signal(barrier, inc=1, device_id={"cols": other}, device_id_type=MESH)
    pl.semaphore_wait(barrier, n_rows + 1)

    def remote(src, dst, s, r, where):
        return pltpu.make_async_remote_copy(
            src_ref=src, dst_ref=dst, send_sem=s, recv_sem=r, device_id=where, device_id_type=MESH
        )

    started = []

    def start(copy):
        copy.start()
        started.append(copy)
        return copy

    def scatter(q, source):
        return [
            start(remote(source.at[theirs + t], rs_buf.at[q, t], rs_s.at[q, t], rs_r.at[q, t], {"cols": sibling}))
            for t in range(per_half)
        ]

    def cross(q, t):
        return start(remote(y_send.at[q, t], y_recv.at[q, t], y_s.at[q, t], y_r.at[q, t], {"cols": across}))

    def hand_over(q, t):
        return start(remote(total.at[q, t], from_sib.at[q, t], ag_s.at[q, t], ag_r.at[q, t], {"cols": sibling}))

    def columns_of(owner):
        return pl.ds(pl.multiple_of(owner * depth, depth), depth)

    def keep(owner, value):
        high, low = split(value)
        d_high[:, columns_of(owner)] = high
        d_low[:, columns_of(owner)] = low

    def keep_slots(h, owner, value):
        high, low = split(value)
        b_both[h, columns_of(owner), :LANES] = high
        b_both[h, columns_of(owner), LANES:] = low

    def multiply_half(h, store):
        tile = cap * b
        right_side = b_both[h]

        def step(i, carry):
            rows = pl.ds(pl.multiple_of(i * tile, tile), tile)
            both = jnp.dot(d_high[rows, :], right_side, preferred_element_type=jnp.float32)
            low = jnp.dot(d_low[rows, :], right_side[:, :LANES], preferred_element_type=jnp.float32)
            store(i, rows, both[:, :LANES] + (both[:, LANES:] + low))
            return carry

        lax.fori_loop(0, rows_all // tile, step, 0)

    list_copies = [
        start(remote(fetch.at[right(k)], lists.at[me], list_s.at[k], list_r.at[k], {"rows": right(k)}))
        for k in range(1, n_rows)
    ]
    h_scatter = scatter(0, dh)
    h_cross, p_cross = [], []
    for t in range(per_half):
        h_scatter[t].wait_recv()
        y_send[0, t] = dh[mine + t] + rs_buf[0, t]
        h_cross.append(cross(0, t))
    p_scatter = scatter(1, dp)
    for copy in list_copies:
        copy.wait_recv()
    lists[me] = fetch[me]
    local = pltpu.make_async_copy(lists, wanted, list_l)
    local.start()
    local.wait()

    def pack(q, h, k, source):
        to = right(k)
        for e in range(cap):
            row = wanted[to, 0, q * cap + e]
            packed[q, h, k, e * b:(e + 1) * b, :] = source(h, row)

    def send_slots(q, h, k):
        return start(
            remote(packed.at[q, h, k], slots.at[q, h, k], slot_s.at[q, h, k], slot_r.at[q, h, k], {"rows": right(k)})
        )

    def panel_rows(h, row):
        return panel[row, :, h * LANES:(h + 1) * LANES]

    def x_rows(h, row):
        return x_buf[h, row]

    panel_copies = {}
    for h in range(halves):
        for k in range(1, n_rows):
            pack(0, h, k, panel_rows)
            panel_copies[h, k] = send_slots(0, h, k)
    for h in range(halves):
        pack(0, h, 0, panel_rows)
        keep_slots(h, me, packed[0, h, 0])

    for t in range(per_half):
        p_scatter[t].wait_recv()
        y_send[1, t] = dp[mine + t] + rs_buf[1, t]

    def finish(q, copies, after):
        handed = []
        for t in range(per_half):
            copies[t].wait_recv()
            total[q, t] = y_send[q, t] + y_recv[q, t]
            handed.append(hand_over(q, t))
            after(t)
            keep(mine + t, total[q, t])
        for t in range(per_half):
            handed[t].wait_recv()
            keep(theirs + t, from_sib[q, t])

    def start_p(t):
        if t >= per_half - 2:
            upto = per_half if t == per_half - 1 else 1
            while len(p_cross) < upto:
                p_cross.append(cross(1, len(p_cross)))

    finish(0, h_cross, start_p)

    x_copies = {}
    for h in range(halves):
        for k in range(1, n_rows):
            panel_copies[h, k].wait_recv()
            keep_slots(h, left(k), slots[0, h, k])

        def store_x(i, rows, value, h=h):
            for e in range(cap):
                x_buf[h, i * cap + e] = value[e * b:(e + 1) * b]

        multiply_half(h, store_x)
        for k in range(1, n_rows):
            pack(1, h, k, x_rows)
            x_copies[h, k] = send_slots(1, h, k)
    for h in range(halves):
        pack(1, h, 0, x_rows)
        keep_slots(h, me, packed[1, h, 0])

    finish(1, p_cross, lambda t: None)

    for h in range(halves):
        for k in range(1, n_rows):
            x_copies[h, k].wait_recv()
            keep_slots(h, left(k), slots[1, h, k])

        def store_w(i, rows, value, h=h):
            out[rows, h * LANES:(h + 1) * LANES] = value

        multiply_half(h, store_w)
    for copy in started:
        copy.wait_send()


def merged_body(n_rows, n_cols, h_blocks, p_blocks, h_fetch, p_fetch, h_slot, p_slot, p_panel):
    cap, b = h_fetch.shape[2], h_blocks.shape[2]
    rows_all, columns = p_panel.shape
    depth, per_half, halves = cap * b, n_rows // 2, columns // LANES
    dh, dp = merge(h_slot, p_slot, h_blocks, p_blocks, n_rows, cap)
    fetch = jnp.concatenate([h_fetch[0], p_fetch[0]], axis=1)
    fetch = jnp.pad(fetch, ((0, 0), (0, LANES - 2 * cap))).reshape(n_rows, 1, LANES)
    f32, bf16, dma = jnp.float32, jnp.bfloat16, pltpu.SemaphoreType.DMA
    exchanged = pltpu.VMEM((2, per_half, rows_all, depth), f32)
    vmem = pl.BlockSpec(memory_space=pltpu.VMEM)
    return pl.pallas_call(
        functools.partial(product_kernel, n_rows, n_cols, cap, b),
        out_shape=jax.ShapeDtypeStruct((rows_all, columns), f32),
        in_specs=[vmem] * 4,
        out_specs=vmem,
        scratch_shapes=[
            pltpu.VMEM((n_rows, 1, LANES), jnp.int32),
            pltpu.SMEM((n_rows, 1, LANES), jnp.int32),
            exchanged, exchanged, exchanged, exchanged, exchanged,
            pltpu.VMEM((rows_all, n_rows * depth), bf16),
            pltpu.VMEM((rows_all, n_rows * depth), bf16),
            pltpu.VMEM((2, halves, n_rows, depth, LANES), f32),
            pltpu.VMEM((2, halves, n_rows, depth, LANES), f32),
            pltpu.VMEM((halves, n_rows * depth, 2 * LANES), bf16),
            pltpu.VMEM((halves, rows_all // b, b, LANES), f32),
            dma((n_rows,)), dma((n_rows,)), dma,
            dma((2, per_half)), dma((2, per_half)),
            dma((2, per_half)), dma((2, per_half)),
            dma((2, per_half)), dma((2, per_half)),
            dma((2, halves, n_rows)), dma((2, halves, n_rows)),
        ],
        compiler_params=pltpu.CompilerParams(
            collective_id=0, has_side_effects=True, vmem_limit_bytes=48 * 1024 * 1024
        ),
        name="product",
    )(dh, dp, fetch, p_panel.reshape(-1, b, columns))


def solution(mesh):
    n_rows, n_cols = mesh.shape["rows"], mesh.shape["cols"]
    in_specs = (
        P("rows", "cols", None, None),
        P("rows", "cols", None, None),
        P("rows", None, None),
        P("rows", None, None),
        P("rows", None),
        P("rows", None),
        P("rows", "cols"),
    )
    out_specs = P("rows", "cols")

    def body(h_blocks, p_blocks, h_fetch, p_fetch, h_slot, p_slot, p_panel):
        cap, b = h_fetch.shape[2], h_blocks.shape[2]
        fits = n_cols == 4 and n_rows % 2 == 0 and cap * b == LANES and h_blocks.shape[0] % cap == 0 and p_panel.shape[1] % LANES == 0
        arguments = (h_blocks, p_blocks, h_fetch, p_fetch, h_slot, p_slot, p_panel)
        if fits and cap * n_rows <= h_slot.shape[1]:
            return merged_body(n_rows, n_cols, *arguments)
        return list_body(*arguments)

    return jax.shard_map(body, mesh=mesh, in_specs=in_specs, out_specs=out_specs, check_vma=False)
```

time: 206 us -> 74.7 us (0.36)
  waiting for transfers between devices: 100 us -> 0 us
  Pallas kernels: 0 us -> 68.7 us
  matrix products: 43.8 us -> 0 us
  starting transfers between devices: 19.7 us -> 0 us
  local copies, waits for them, and re-layouts: 24.8 us -> 5.49 us
  between operations: 13.5 us -> 0.02 us
  other arithmetic: 3.68 us -> 0.08 us
    pallas_call x0 -> x2, Pallas kernels: none -> 68.7 us  [the longest x1 59.8 us: merged_body(): pl.pallas_call(functools.partial(product_kernel, n_rows, n_cols, cap, b),...]
    all_to_all x4 -> x0, waiting for transfers between devices: 57.2 us -> none  [the longest x2 47.8 us: multiply(): lax.all_to_all(packed, 'rows', split_axis=0, concat_axis=0, tiled=True)]
    dot_general x2 -> x0, matrix products: 43.8 us -> none  [multiply(): result = jnp.einsum('ijab,ijbc->iac', block_list, chosen, precision=highest)]
    all_gather x2 -> x0, waiting for transfers between devices: 41.8 us -> none  [the longest x1 23.9 us: body(): lax.all_gather(h_blocks, 'cols', axis=1, tiled=True)]
    gather x4 -> x0, local copies, waits for them, and re-layouts: 21.2 us -> none  [the longest x2 20 us: multiply(): chosen = jnp.take(flattened, slot_lists, axis=0)]
    all_to_all x4 -> x0, starting transfers between devices: 19.6 us -> none  [the longest x2 10.5 us: multiply(): lax.all_to_all(fetch_lists[0], 'rows', split_axis=0, concat_axis=0, tiled...]
    unnamed x6 -> x7, local copies, waits for them, and re-layouts: 0.01 us -> 3.98 us
    select_n x6 -> x0, other arithmetic: 2.94 us -> none  [the longest x4 2.24 us: multiply(): packed = jnp.take(stacked, wanted, axis=0)]
  transfers between devices with their start and end apart: 6 -> 0, of which waited for: 6 -> 0; matrix products, arithmetic and copies ran while one was open for 25% -> 0% of each run, Pallas kernels for 0% -> 0%
where the time goes in v1:
time: 74.7 us; the launch traced here: 74.3 us
  Pallas kernels  68.7 us (92%)
  local copies, waits for them, and re-layouts  5.49 us (7%)
    pallas_call x1, Pallas kernels, merged_body(): pl.pallas_call(functools.partial(product_kernel, n_rows, n_cols, cap, b),...  59.8 us
    pallas_call x1, Pallas kernels, merge(): pl.pallas_call(functools.partial(merge_kernel, cap), out_shape=(shape, sh...  8.86 us
    unnamed x7, local copies, waits for them, and re-layouts  3.98 us
    squeeze x2, local copies, waits for them, and re-layouts, merged_body(): fetch = jnp.concatenate([h_fetch[0], p_fetch[0]], axis=1)  1.51 us

profile of v1, /device:TPU:0, one launch (start us, length us, event | category | flops | bytes accessed | tf_op | source)
XLA Modules:
  0.0 74.3 jit_solution(114027635351638096)
XLA Ops:
  0.0 0.8 %copy.8 = s32[8,2]{1,0:T(8,128)S(1)} copy(s32[8,2]{0,1:T(2,128)} %bitcast.6) | data formatting | bytes 128 | tf_op jit(solution)/shard_map/squeeze | solution.py:280
  0.8 0.8 %copy.9 = s32[8,2]{1,0:T(8,128)S(1)} copy(s32[8,2]{0,1:T(2,128)} %bitcast.7) | data formatting | bytes 128 | tf_op jit(solution)/shard_map/squeeze | solution.py:280
  1.5 0.1 pad_add_fusion
  1.6 0.0 copy-start.2
  1.6 8.9 %merge.1 = (f32[8,512,128]{2,1,0:T(8,128)}, f32[8,512,128]{2,1,0:T(8,128)}) custom-call(s32[8,48]{1,0:T(8,128)} %h_slot.1, s32[8,48]{1,0:T(8,128)} %p_slot.1, f32[8,12,64,64]{3,2,1,0:T(8,128)} %h_blocks.1, f32[8,12,64,64]{3,2,1,0:T(8,128)} %p_blocks.1), custom_call_target="tpu_custom_call" | custom-call | tf_op jit(solution)/shard_map/merge/pallas_call | solution.py:79
  10.5 0.0 copy-done.2
  10.5 0.0 copy-start
  10.5 1.6 %copy-done = f32[8,512,128]{2,1,0:T(8,128)S(1)} copy-done((f32[8,512,128]{2,1,0:T(8,128)S(1)}, f32[8,512,128]{2,1,0:T(8,128)}, u32[]{:S(2)}) %copy-start) | copy-done | bytes 2097176
  12.0 0.0 copy-start.1
  12.0 1.6 %copy-done.1 = f32[8,512,128]{2,1,0:T(8,128)S(1)} copy-done((f32[8,512,128]{2,1,0:T(8,128)S(1)}, f32[8,512,128]{2,1,0:T(8,128)}, u32[]{:S(2)}) %copy-start.1) | copy-done | bytes 2097176
  13.6 59.8 %product.1 = f32[512,256]{1,0:T(8,128)S(1)} custom-call(f32[8,512,128]{2,1,0:T(8,128)S(1)} %copy-done, f32[8,512,128]{2,1,0:T(8,128)S(1)} %copy-done.1, s32[8,1,128]{2,1,0:T(1,128)S(1)} %bitcast.5, f32[8,64,256]{2,1,0:T(8,128)S(1)} %bitcast.4), custom_call_target="tpu_custom_call" | custom-call | tf_op jit(solution)/shard_map/product/pallas_call | solution.py:285
  73.5 0.8 %copy.11 = f32[512,256]{1,0:T(8,128)} copy(f32[512,256]{1,0:T(8,128)S(1)} %product.1) | data formatting | bytes 1048576
  (1 shorter events, 0.0 us)
Async XLA Ops:
  1.6 8.9 %copy-start.2 = (f32[512,256]{1,0:T(8,128)S(1)}, f32[512,256]{1,0:T(8,128)}, u32[]{:S(2)}) copy-start(f32[512,256]{1,0:T(8,128)} %param.13) | copy-start | bytes 1572868
  10.5 1.6 %copy-start = (f32[8,512,128]{2,1,0:T(8,128)S(1)}, f32[8,512,128]{2,1,0:T(8,128)}, u32[]{:S(2)}) copy-start(f32[8,512,128]{2,1,0:T(8,128)} %get-tuple-element.7.dh) | copy-start | bytes 6291460
  12.0 1.6 %copy-start.1 = (f32[8,512,128]{2,1,0:T(8,128)S(1)}, f32[8,512,128]{2,1,0:T(8,128)}, u32[]{:S(2)}) copy-start(f32[8,512,128]{2,1,0:T(8,128)} %get-tuple-element.8.dp) | copy-start | bytes 6291460

commit v2 on v1

--- a/solution.py
+++ b/solution.py
@@ -56,36 +56,6 @@
     return multiply(gathered[1], p_fetch, p_slot, middle)
 
 
-def merge_kernel(cap, h_slot, p_slot, h_blocks, p_blocks, h_out, p_out):
-    i = pl.program_id(0)
-    n_local, b = h_blocks.shape[1], h_blocks.shape[2]
-    first = lax.axis_index("cols") * n_local
-    lane_part = lax.broadcasted_iota(jnp.int32, (b, cap * b), 1) // b
-    for slots, blocks, out in ((h_slot, h_blocks, h_out), (p_slot, p_blocks, p_out)):
-        out[...] = jnp.zeros_like(out)
-        for j in range(n_local):
-            slot = slots[i, first + j]
-            owner, part = slot // cap, slot % cap
-            block = blocks[0, j]
-            wide = jnp.concatenate([block] * cap, axis=1)
-            out[owner] += jnp.where(lane_part == part, wide, 0.0)
-
-
-def merge(h_slot, p_slot, h_blocks, p_blocks, n_rows, cap):
-    own_rows, n_local, b, _ = h_blocks.shape
-    blocks = pl.BlockSpec((1, n_local, b, b), lambda i, *_: (i, 0, 0, 0))
-    merged = pl.BlockSpec((n_rows, b, cap * b), lambda i, *_: (0, i, 0))
-    shape = jax.ShapeDtypeStruct((n_rows, own_rows * b, cap * b), jnp.float32)
-    return pl.pallas_call(
-        functools.partial(merge_kernel, cap),
-        out_shape=(shape, shape),
-        grid_spec=pltpu.PrefetchScalarGridSpec(
-            num_scalar_prefetch=2, grid=(own_rows,), in_specs=[blocks, blocks], out_specs=[merged, merged]
-        ),
-        name="merge",
-    )(h_slot, p_slot, h_blocks, p_blocks)
-
-
 def split(x):
     high = x.astype(jnp.bfloat16)
     return high, (x - high.astype(jnp.float32)).astype(jnp.bfloat16)
@@ -93,10 +63,10 @@
 
 def product_kernel(
     n_rows, n_cols, cap, b,
-    dh, dp, fetch, panel, out,
-    lists, wanted, rs_buf, y_send, y_recv, total, from_sib, d_high, d_low,
+    h_slot, p_slot, h_fetch, p_fetch, h_blocks, p_blocks, panel, out,
+    blocks, merged, message, lists, wanted, rs_buf, y_send, y_recv, total, from_sib, d_high, d_low,
     packed, slots, b_both, x_buf,
-    list_s, list_r, list_l, rs_s, rs_r, y_s, y_r, ag_s, ag_r, slot_s, slot_r,
+    load_s, list_s, list_r, list_l, rs_s, rs_r, y_s, y_r, ag_s, ag_r, slot_s, slot_r,
 ):
     me, c = lax.axis_index("rows"), lax.axis_index("cols")
     core = lax.rem(c, 2)
@@ -114,11 +84,46 @@
     def left(k):
         return lax.rem(me + n_rows - k, n_rows)
 
+    loads = [pltpu.make_async_copy(source, blocks.at[q], load_s.at[q]) for q, source in enumerate((h_blocks, p_blocks))]
+    for load in loads:
+        load.start()
+    slot_lists = (h_slot, p_slot)
+    own_rows, n_local = blocks.shape[1:3]
+    lane_part = lax.broadcasted_iota(jnp.int32, (8, depth), 1) // b
+
+    def merge(q, first_owner):
+        slot_list = slot_lists[q]
+
+        def step(i, carry):
+            sums = [jnp.zeros((b // 8, 8, depth), jnp.float32)] * per_half
+            for j in range(n_local):
+                slot = slot_list[i, c * n_local + j] - first_owner * cap
+                block = blocks[q, i, j]
+                wide = jnp.concatenate([block] * cap, axis=1).reshape(b // 8, 8, depth)
+                for t in range(per_half):
+                    named = (lane_part == slot - t * cap)[None]
+                    sums[t] = sums[t] + jnp.where(named, wide, 0.0)
+            rows = pl.ds(pl.multiple_of(i * b, b), b)
+            for t in range(per_half):
+                merged[q, first_owner + t, rows, :] = sums[t].reshape(b, depth)
+            return carry
+
+        lax.fori_loop(0, own_rows, step, 0)
+
     barrier = pltpu.get_barrier_semaphore()
     for k in range(1, n_rows):
         pl.semaphore_signal(barrier, inc=1, device_id={"rows": right(k)}, device_id_type=MESH)
     for other in (sibling, across):
         pl.semaphore_signal(barrier, inc=1, device_id={"cols": other}, device_id_type=MESH)
+    lane = lax.broadcasted_iota(jnp.int32, (1, LANES), 1)
+    for o in range(n_rows):
+        row = jnp.zeros((1, LANES), jnp.int32)
+        for q, fetch in enumerate((h_fetch, p_fetch)):
+            for e in range(cap):
+                row = jnp.where(lane == q * cap + e, fetch[0, e, o], row)
+        message[o] = row
+    loads[0].wait()
+    merge(0, theirs)
     pl.semaphore_wait(barrier, n_rows + 1)
 
     def remote(src, dst, s, r, where):
@@ -133,9 +138,9 @@
         started.append(copy)
         return copy
 
-    def scatter(q, source):
+    def scatter(q):
         return [
-            start(remote(source.at[theirs + t], rs_buf.at[q, t], rs_s.at[q, t], rs_r.at[q, t], {"cols": sibling}))
+            start(remote(merged.at[q, theirs + t], rs_buf.at[q, t], rs_s.at[q, t], rs_r.at[q, t], {"cols": sibling}))
             for t in range(per_half)
         ]
 
@@ -172,19 +177,19 @@
         lax.fori_loop(0, rows_all // tile, step, 0)
 
     list_copies = [
-        start(remote(fetch.at[right(k)], lists.at[me], list_s.at[k], list_r.at[k], {"rows": right(k)}))
+        start(remote(message.at[right(k)], lists.at[me], list_s.at[k], list_r.at[k], {"rows": right(k)}))
         for k in range(1, n_rows)
     ]
-    h_scatter = scatter(0, dh)
+    h_scatter = scatter(0)
+    merge(0, mine)
     h_cross, p_cross = [], []
     for t in range(per_half):
         h_scatter[t].wait_recv()
-        y_send[0, t] = dh[mine + t] + rs_buf[0, t]
+        y_send[0, t] = merged[0, mine + t] + rs_buf[0, t]
         h_cross.append(cross(0, t))
-    p_scatter = scatter(1, dp)
     for copy in list_copies:
         copy.wait_recv()
-    lists[me] = fetch[me]
+    lists[me] = message[me]
     local = pltpu.make_async_copy(lists, wanted, list_l)
     local.start()
     local.wait()
@@ -215,9 +220,13 @@
         pack(0, h, 0, panel_rows)
         keep_slots(h, me, packed[0, h, 0])
 
+    loads[1].wait()
+    merge(1, theirs)
+    p_scatter = scatter(1)
+    merge(1, mine)
     for t in range(per_half):
         p_scatter[t].wait_recv()
-        y_send[1, t] = dp[mine + t] + rs_buf[1, t]
+        y_send[1, t] = merged[1, mine + t] + rs_buf[1, t]
 
     def finish(q, copies, after):
         handed = []
@@ -276,18 +285,19 @@
     cap, b = h_fetch.shape[2], h_blocks.shape[2]
     rows_all, columns = p_panel.shape
     depth, per_half, halves = cap * b, n_rows // 2, columns // LANES
-    dh, dp = merge(h_slot, p_slot, h_blocks, p_blocks, n_rows, cap)
-    fetch = jnp.concatenate([h_fetch[0], p_fetch[0]], axis=1)
-    fetch = jnp.pad(fetch, ((0, 0), (0, LANES - 2 * cap))).reshape(n_rows, 1, LANES)
     f32, bf16, dma = jnp.float32, jnp.bfloat16, pltpu.SemaphoreType.DMA
     exchanged = pltpu.VMEM((2, per_half, rows_all, depth), f32)
-    vmem = pl.BlockSpec(memory_space=pltpu.VMEM)
+    slots_and_lists = (h_slot, p_slot, jnp.swapaxes(h_fetch, 1, 2), jnp.swapaxes(p_fetch, 1, 2))
+    vmem, smem = pl.BlockSpec(memory_space=pltpu.VMEM), pl.BlockSpec(memory_space=pltpu.SMEM)
     return pl.pallas_call(
         functools.partial(product_kernel, n_rows, n_cols, cap, b),
         out_shape=jax.ShapeDtypeStruct((rows_all, columns), f32),
-        in_specs=[vmem] * 4,
+        in_specs=[smem] * 4 + [pl.BlockSpec(memory_space=pltpu.HBM)] * 2 + [vmem],
         out_specs=vmem,
         scratch_shapes=[
+            pltpu.VMEM((2, *h_blocks.shape), f32),
+            pltpu.VMEM((2, n_rows, rows_all, depth), f32),
+            pltpu.VMEM((n_rows, 1, LANES), jnp.int32),
             pltpu.VMEM((n_rows, 1, LANES), jnp.int32),
             pltpu.SMEM((n_rows, 1, LANES), jnp.int32),
             exchanged, exchanged, exchanged, exchanged, exchanged,
@@ -297,7 +307,7 @@
             pltpu.VMEM((2, halves, n_rows, depth, LANES), f32),
             pltpu.VMEM((halves, n_rows * depth, 2 * LANES), bf16),
             pltpu.VMEM((halves, rows_all // b, b, LANES), f32),
-            dma((n_rows,)), dma((n_rows,)), dma,
+            dma((2,)), dma((n_rows,)), dma((n_rows,)), dma,
             dma((2, per_half)), dma((2, per_half)),
             dma((2, per_half)), dma((2, per_half)),
             dma((2, per_half)), dma((2, per_half)),
@@ -307,7 +317,7 @@
             collective_id=0, has_side_effects=True, vmem_limit_bytes=48 * 1024 * 1024
         ),
         name="product",
-    )(dh, dp, fetch, p_panel.reshape(-1, b, columns))
+    )(*slots_and_lists, h_blocks, p_blocks, p_panel.reshape(-1, b, columns))
 
 
 def solution(mesh):

time: 74.7 us -> 67.7 us (0.906)
  Pallas kernels: 68.7 us -> 60.3 us
  local copies, waits for them, and re-layouts: 5.49 us -> 6.46 us
    pallas_call x1 -> x0, Pallas kernels: 8.86 us -> none  [merge(): pl.pallas_call(functools.partial(merge_kernel, cap), out_shape=(shape, sh...]
    unnamed x7 -> x13, local copies, waits for them, and re-layouts: 3.98 us -> 6.46 us
    squeeze x2 -> x0, local copies, waits for them, and re-layouts: 1.51 us -> none  [merged_body(): fetch = jnp.concatenate([h_fetch[0], p_fetch[0]], axis=1)]
where the time goes in v2:
time: 67.7 us; the launch traced here: 66.8 us
  Pallas kernels  60.3 us (89%)
  local copies, waits for them, and re-layouts  6.46 us (10%)
    pallas_call x1, Pallas kernels, merged_body(): pl.pallas_call(functools.partial(product_kernel, n_rows, n_cols, cap, b),...  60.3 us
    unnamed x13, local copies, waits for them, and re-layouts  6.46 us

profile of v2, /device:TPU:0, one launch (start us, length us, event | category | flops | bytes accessed | tf_op | source)
XLA Modules:
  0.0 66.8 jit_solution(8353268881648375852)
XLA Ops:
  0.0 0.0 copy-start
  0.0 1.9 %copy-done = f32[8,12,64,64]{3,2,1,0:T(8,128)S(1)} copy-done((f32[8,12,64,64]{3,2,1,0:T(8,128)S(1)}, f32[8,12,64,64]{3,2,1,0:T(8,128)}, u32[]{:S(2)}) %copy-start) | copy-done | bytes 1572888
  1.9 0.0 copy-start.1
  1.9 1.0 %copy-done.1 = f32[512,256]{1,0:T(8,128)S(1)} copy-done((f32[512,256]{1,0:T(8,128)S(1)}, f32[512,256]{1,0:T(8,128)}, u32[]{:S(2)}) %copy-start.1) | copy-done | bytes 524312
  2.9 0.0 copy-start.2
  2.9 0.7 %copy-done.2 = s32[8,48]{1,0:T(8,128)S(1)} copy-done((s32[8,48]{1,0:T(8,128)S(1)}, s32[8,48]{1,0:T(8,128)}, u32[]{:S(2)}) %copy-start.2) | copy-done | bytes 1560
  3.6 0.0 copy-start.3
  3.6 0.7 %copy-done.3 = s32[8,48]{1,0:T(8,128)S(1)} copy-done((s32[8,48]{1,0:T(8,128)S(1)}, s32[8,48]{1,0:T(8,128)}, u32[]{:S(2)}) %copy-start.3) | copy-done | bytes 1560
  4.3 0.0 copy-start.4
  4.3 0.7 %copy-done.4 = s32[1,8,2]{1,2,0:T(2,128)S(1)} copy-done((s32[1,8,2]{1,2,0:T(2,128)S(1)}, s32[1,8,2]{1,2,0:T(2,128)}, u32[]{:S(2)}) %copy-start.4) | copy-done | bytes 88
  5.0 0.0 copy-start.5
  5.0 0.7 %copy-done.5 = s32[1,8,2]{1,2,0:T(2,128)S(1)} copy-done((s32[1,8,2]{1,2,0:T(2,128)S(1)}, s32[1,8,2]{1,2,0:T(2,128)}, u32[]{:S(2)}) %copy-start.5) | copy-done | bytes 88
  5.7 60.3 %product.1 = f32[512,256]{1,0:T(8,128)S(1)} custom-call(s32[8,48]{1,0:T(8,128)S(1)} %copy-done.2, s32[8,48]{1,0:T(8,128)S(1)} %copy-done.3, s32[1,2,8]{2,1,0:T(2,128)S(1)} %bitcast.4, s32[1,2,8]{2,1,0:T(2,128)S(1)} %bitcast.5, f32[8,12,64,64]{3,2,1,0:T(8,128)S(1)} %copy-done, f32[8,12,64,64]{3,2,1,0:T(8,128)} %p_blocks.1, f32[8,64,256]{2,1,0:T(8,128)S(1)} %bitcast.3), custom_call_target="tpu_custom_call" | custom-call | tf_op jit(solution)/shard_map/product/pallas_call | solution.py:292
  66.0 0.8 %copy.9 = f32[512,256]{1,0:T(8,128)} copy(f32[512,256]{1,0:T(8,128)S(1)} %product.1) | data formatting | bytes 1048576
Async XLA Ops:
  0.0 1.9 %copy-start = (f32[8,12,64,64]{3,2,1,0:T(8,128)S(1)}, f32[8,12,64,64]{3,2,1,0:T(8,128)}, u32[]{:S(2)}) copy-start(f32[8,12,64,64]{3,2,1,0:T(8,128)} %h_blocks.1) | copy-start | bytes 4718596
  1.9 1.0 %copy-start.1 = (f32[512,256]{1,0:T(8,128)S(1)}, f32[512,256]{1,0:T(8,128)}, u32[]{:S(2)}) copy-start(f32[512,256]{1,0:T(8,128)} %param.13) | copy-start | bytes 1572868
  2.9 0.7 %copy-start.2 = (s32[8,48]{1,0:T(8,128)S(1)}, s32[8,48]{1,0:T(8,128)}, u32[]{:S(2)}) copy-start(s32[8,48]{1,0:T(8,128)} %h_slot.1) | copy-start | bytes 4612
  3.6 0.7 %copy-start.3 = (s32[8,48]{1,0:T(8,128)S(1)}, s32[8,48]{1,0:T(8,128)}, u32[]{:S(2)}) copy-start(s32[8,48]{1,0:T(8,128)} %p_slot.1) | copy-start | bytes 4612
  4.3 0.7 %copy-start.4 = (s32[1,8,2]{1,2,0:T(2,128)S(1)}, s32[1,8,2]{1,2,0:T(2,128)}, u32[]{:S(2)}) copy-start(s32[1,8,2]{1,2,0:T(2,128)} %param.9) | copy-start | bytes 196
  5.0 0.7 %copy-start.5 = (s32[1,8,2]{1,2,0:T(2,128)S(1)}, s32[1,8,2]{1,2,0:T(2,128)}, u32[]{:S(2)}) copy-start(s32[1,8,2]{1,2,0:T(2,128)} %param.10) | copy-start | bytes 196

commit v3 on v2

--- a/solution.py
+++ b/solution.py
@@ -65,7 +65,7 @@
     n_rows, n_cols, cap, b,
     h_slot, p_slot, h_fetch, p_fetch, h_blocks, p_blocks, panel, out,
     blocks, merged, message, lists, wanted, rs_buf, y_send, y_recv, total, from_sib, d_high, d_low,
-    packed, slots, b_both, x_buf,
+    packed, slots, b_high, b_low, x_buf,
     load_s, list_s, list_r, list_l, rs_s, rs_r, y_s, y_r, ag_s, ag_r, slot_s, slot_r,
 ):
     me, c = lax.axis_index("rows"), lax.axis_index("cols")
@@ -84,14 +84,21 @@
     def left(k):
         return lax.rem(me + n_rows - k, n_rows)
 
-    loads = [pltpu.make_async_copy(source, blocks.at[q], load_s.at[q]) for q, source in enumerate((h_blocks, p_blocks))]
-    for load in loads:
-        load.start()
+    tile = cap * b
+    tiles = rows_all // tile
+
+    def load(q, t):
+        some = pl.ds(t * cap, cap)
+        return pltpu.make_async_copy((h_blocks, p_blocks)[q].at[some], blocks.at[q, some], load_s.at[q, t])
+
+    for q in range(2):
+        for t in range(tiles):
+            load(q, t).start()
     slot_lists = (h_slot, p_slot)
     own_rows, n_local = blocks.shape[1:3]
     lane_part = lax.broadcasted_iota(jnp.int32, (8, depth), 1) // b
 
-    def merge(q, first_owner):
+    def merge(q, first_owner, start_row, end_row):
         slot_list = slot_lists[q]
 
         def step(i, carry):
@@ -108,7 +115,7 @@
                 merged[q, first_owner + t, rows, :] = sums[t].reshape(b, depth)
             return carry
 
-        lax.fori_loop(0, own_rows, step, 0)
+        lax.fori_loop(start_row, end_row, step, 0)
 
     barrier = pltpu.get_barrier_semaphore()
     for k in range(1, n_rows):
@@ -122,8 +129,9 @@
             for e in range(cap):
                 row = jnp.where(lane == q * cap + e, fetch[0, e, o], row)
         message[o] = row
-    loads[0].wait()
-    merge(0, theirs)
+    for t in range(tiles):
+        load(0, t).wait()
+    merge(0, theirs, 0, own_rows)
     pl.semaphore_wait(barrier, n_rows + 1)
 
     def remote(src, dst, s, r, where):
@@ -138,54 +146,57 @@
         started.append(copy)
         return copy
 
+    def rows_of(t):
+        return pl.ds(t * tile, tile)
+
     def scatter(q):
+        source = merged.at[q, pl.ds(theirs, per_half)]
         return [
-            start(remote(merged.at[q, theirs + t], rs_buf.at[q, t], rs_s.at[q, t], rs_r.at[q, t], {"cols": sibling}))
-            for t in range(per_half)
+            start(remote(source.at[:, rows_of(t)], rs_buf.at[q, :, rows_of(t)], rs_s.at[q, t], rs_r.at[q, t], {"cols": sibling}))
+            for t in range(tiles)
         ]
 
+    def add_cores(q, t, arriving):
+        arriving.wait_recv()
+        y_send[q, :, rows_of(t)] = merged[q, pl.ds(mine, per_half), rows_of(t)] + rs_buf[q, :, rows_of(t)]
+
     def cross(q, t):
-        return start(remote(y_send.at[q, t], y_recv.at[q, t], y_s.at[q, t], y_r.at[q, t], {"cols": across}))
+        part = (q, slice(None), rows_of(t))
+        return start(remote(y_send.at[part], y_recv.at[part], y_s.at[q, t], y_r.at[q, t], {"cols": across}))
 
     def hand_over(q, t):
-        return start(remote(total.at[q, t], from_sib.at[q, t], ag_s.at[q, t], ag_r.at[q, t], {"cols": sibling}))
+        part = (q, slice(None), rows_of(t))
+        return start(remote(total.at[part], from_sib.at[part], ag_s.at[q, t], ag_r.at[q, t], {"cols": sibling}))
 
     def columns_of(owner):
         return pl.ds(pl.multiple_of(owner * depth, depth), depth)
 
-    def keep(owner, value):
-        high, low = split(value)
-        d_high[:, columns_of(owner)] = high
-        d_low[:, columns_of(owner)] = low
+    def keep(first_owner, t, value):
+        for o in range(per_half):
+            high, low = split(value[o])
+            d_high[rows_of(t), columns_of(first_owner + o)] = high
+            d_low[rows_of(t), columns_of(first_owner + o)] = low
 
     def keep_slots(h, owner, value):
         high, low = split(value)
-        b_both[h, columns_of(owner), :LANES] = high
-        b_both[h, columns_of(owner), LANES:] = low
-
-    def multiply_half(h, store):
-        tile = cap * b
-        right_side = b_both[h]
-
-        def step(i, carry):
-            rows = pl.ds(pl.multiple_of(i * tile, tile), tile)
-            both = jnp.dot(d_high[rows, :], right_side, preferred_element_type=jnp.float32)
-            low = jnp.dot(d_low[rows, :], right_side[:, :LANES], preferred_element_type=jnp.float32)
-            store(i, rows, both[:, :LANES] + (both[:, LANES:] + low))
-            return carry
-
-        lax.fori_loop(0, rows_all // tile, step, 0)
+        b_high[columns_of(owner), h * LANES:(h + 1) * LANES] = high
+        b_low[columns_of(owner), h * LANES:(h + 1) * LANES] = low
+
+    def multiply_tile(rows, lanes):
+        f32 = jnp.float32
+        high = jnp.dot(d_high[rows, :], b_high[:, lanes], preferred_element_type=f32)
+        cross_terms = jnp.dot(d_high[rows, :], b_low[:, lanes], preferred_element_type=f32)
+        return high + (cross_terms + jnp.dot(d_low[rows, :], b_high[:, lanes], preferred_element_type=f32))
 
     list_copies = [
         start(remote(message.at[right(k)], lists.at[me], list_s.at[k], list_r.at[k], {"rows": right(k)}))
         for k in range(1, n_rows)
     ]
     h_scatter = scatter(0)
-    merge(0, mine)
     h_cross, p_cross = [], []
-    for t in range(per_half):
-        h_scatter[t].wait_recv()
-        y_send[0, t] = merged[0, mine + t] + rs_buf[0, t]
+    for t in range(tiles):
+        merge(0, mine, t * cap, (t + 1) * cap)
+        add_cores(0, t, h_scatter[t])
         h_cross.append(cross(0, t))
     for copy in list_copies:
         copy.wait_recv()
@@ -220,45 +231,49 @@
         pack(0, h, 0, panel_rows)
         keep_slots(h, me, packed[0, h, 0])
 
-    loads[1].wait()
-    merge(1, theirs)
+    for t in range(tiles):
+        load(1, t).wait()
+    merge(1, theirs, 0, own_rows)
     p_scatter = scatter(1)
-    merge(1, mine)
-    for t in range(per_half):
-        p_scatter[t].wait_recv()
-        y_send[1, t] = merged[1, mine + t] + rs_buf[1, t]
-
-    def finish(q, copies, after):
-        handed = []
-        for t in range(per_half):
-            copies[t].wait_recv()
-            total[q, t] = y_send[q, t] + y_recv[q, t]
-            handed.append(hand_over(q, t))
-            after(t)
-            keep(mine + t, total[q, t])
-        for t in range(per_half):
-            handed[t].wait_recv()
-            keep(theirs + t, from_sib[q, t])
-
-    def start_p(t):
-        if t >= per_half - 2:
-            upto = per_half if t == per_half - 1 else 1
-            while len(p_cross) < upto:
-                p_cross.append(cross(1, len(p_cross)))
-
-    finish(0, h_cross, start_p)
-
-    x_copies = {}
+    merge(1, mine, 0, own_rows)
+    for t in range(tiles):
+        add_cores(1, t, p_scatter[t])
+
+    def arrive(q, t, crossing):
+        crossing.wait_recv()
+        part = (q, slice(None), rows_of(t))
+        total[part] = y_send[part] + y_recv[part]
+        handed = hand_over(q, t)
+        return handed
+
+    def take_sibling(q, t, handed):
+        handed.wait_recv()
+        keep(theirs, t, from_sib[q, :, rows_of(t)])
+
+    handed = []
+    for t in range(tiles):
+        handed.append(arrive(0, t, h_cross[t]))
+        if t == tiles - 2:
+            p_cross.append(cross(1, 0))
+        if t == tiles - 1:
+            p_cross += [cross(1, u) for u in range(len(p_cross), tiles)]
+        keep(mine, t, total[0, :, rows_of(t)])
+        if t > 0:
+            take_sibling(0, t - 1, handed[t - 1])
+
     for h in range(halves):
         for k in range(1, n_rows):
             panel_copies[h, k].wait_recv()
             keep_slots(h, left(k), slots[0, h, k])
-
-        def store_x(i, rows, value, h=h):
-            for e in range(cap):
-                x_buf[h, i * cap + e] = value[e * b:(e + 1) * b]
-
-        multiply_half(h, store_x)
+    for t in range(tiles):
+        if t == tiles - 1:
+            take_sibling(0, t, handed[t])
+        value = multiply_tile(rows_of(t), slice(None))
+        for e in range(cap):
+            for h in range(halves):
+                x_buf[h, t * cap + e] = value[e * b:(e + 1) * b, h * LANES:(h + 1) * LANES]
+    x_copies = {}
+    for h in range(halves):
         for k in range(1, n_rows):
             pack(1, h, k, x_rows)
             x_copies[h, k] = send_slots(1, h, k)
@@ -266,17 +281,20 @@
         pack(1, h, 0, x_rows)
         keep_slots(h, me, packed[1, h, 0])
 
-    finish(1, p_cross, lambda t: None)
-
-    for h in range(halves):
+    handed = []
+    for t in range(tiles):
+        handed.append(arrive(1, t, p_cross[t]))
+        keep(mine, t, total[1, :, rows_of(t)])
+    for t in range(tiles):
+        take_sibling(1, t, handed[t])
+
+    for h in range(halves):
+        lanes = slice(h * LANES, (h + 1) * LANES)
         for k in range(1, n_rows):
             x_copies[h, k].wait_recv()
             keep_slots(h, left(k), slots[1, h, k])
-
-        def store_w(i, rows, value, h=h):
-            out[rows, h * LANES:(h + 1) * LANES] = value
-
-        multiply_half(h, store_w)
+        for t in range(tiles):
+            out[rows_of(t), lanes] = multiply_tile(rows_of(t), lanes)
     for copy in started:
         copy.wait_send()
 
@@ -285,6 +303,7 @@
     cap, b = h_fetch.shape[2], h_blocks.shape[2]
     rows_all, columns = p_panel.shape
     depth, per_half, halves = cap * b, n_rows // 2, columns // LANES
+    tiles = rows_all // depth
     f32, bf16, dma = jnp.float32, jnp.bfloat16, pltpu.SemaphoreType.DMA
     exchanged = pltpu.VMEM((2, per_half, rows_all, depth), f32)
     slots_and_lists = (h_slot, p_slot, jnp.swapaxes(h_fetch, 1, 2), jnp.swapaxes(p_fetch, 1, 2))
@@ -305,16 +324,17 @@
             pltpu.VMEM((rows_all, n_rows * depth), bf16),
             pltpu.VMEM((2, halves, n_rows, depth, LANES), f32),
             pltpu.VMEM((2, halves, n_rows, depth, LANES), f32),
-            pltpu.VMEM((halves, n_rows * depth, 2 * LANES), bf16),
+            pltpu.VMEM((n_rows * depth, columns), bf16),
+            pltpu.VMEM((n_rows * depth, columns), bf16),
             pltpu.VMEM((halves, rows_all // b, b, LANES), f32),
-            dma((2,)), dma((n_rows,)), dma((n_rows,)), dma,
-            dma((2, per_half)), dma((2, per_half)),
-            dma((2, per_half)), dma((2, per_half)),
-            dma((2, per_half)), dma((2, per_half)),
+            dma((2, tiles)), dma((n_rows,)), dma((n_rows,)), dma,
+            dma((2, tiles)), dma((2, tiles)),
+            dma((2, tiles)), dma((2, tiles)),
+            dma((2, tiles)), dma((2, tiles)),
             dma((2, halves, n_rows)), dma((2, halves, n_rows)),
         ],
         compiler_params=pltpu.CompilerParams(
-            collective_id=0, has_side_effects=True, vmem_limit_bytes=48 * 1024 * 1024
+            collective_id=0, has_side_effects=True, vmem_limit_bytes=58 * 1024 * 1024
         ),
         name="product",
     )(*slots_and_lists, h_blocks, p_blocks, p_panel.reshape(-1, b, columns))

time: 67.7 us -> 63.4 us (0.936)
  local copies, waits for them, and re-layouts: 6.46 us -> 1.87 us
  Pallas kernels: 60.3 us -> 61.1 us
    unnamed x13 -> x1, local copies, waits for them, and re-layouts: 6.46 us -> 1.87 us
    pallas_call x1, Pallas kernels: 60.3 us -> 61.1 us  [merged_body(): pl.pallas_call(functools.partial(product_kernel, n_rows, n_cols, cap, b),...]
where the time goes in v3:
time: 63.4 us; the launch traced here: 63 us
  Pallas kernels  61.1 us (96%)
  local copies, waits for them, and re-layouts  1.87 us (3%)
    pallas_call x1, Pallas kernels, merged_body(): pl.pallas_call(functools.partial(product_kernel, n_rows, n_cols, cap, b),...  61.1 us
    unnamed x1, local copies, waits for them, and re-layouts  1.87 us

profile of v3, /device:TPU:0, one launch (start us, length us, event | category | flops | bytes accessed | tf_op | source)
XLA Modules:
  0.0 63.0 jit_solution(4695859564044103135)
XLA Ops:
  0.0 61.1 %product.1 = f32[512,256]{1,0:T(8,128)} custom-call(s32[8,48]{1,0:T(8,128)} %h_slot.1, s32[8,48]{1,0:T(8,128)} %p_slot.1, s32[1,2,8]{2,1,0:T(2,128)} %bitcast.4, s32[1,2,8]{2,1,0:T(2,128)} %bitcast.5, f32[8,12,64,64]{3,2,1,0:T(8,128)} %h_blocks.1, f32[8,12,64,64]{3,2,1,0:T(8,128)} %p_blocks.1, f32[8,64,256]{2,1,0:T(8,128)} %bitcast.3), custom_call_target="tpu_custom_call" | custom-call | tf_op jit(solution)/shard_map/product/pallas_call | solution.py:311
  61.1 1.9 %copy.9 = f32[512,256]{1,0:T(8,128)} copy(f32[512,256]{1,0:T(8,128)} %product.1) | data formatting | bytes 1048576

commit v4 on v3

--- a/solution.py
+++ b/solution.py
@@ -91,9 +91,8 @@
         some = pl.ds(t * cap, cap)
         return pltpu.make_async_copy((h_blocks, p_blocks)[q].at[some], blocks.at[q, some], load_s.at[q, t])
 
-    for q in range(2):
-        for t in range(tiles):
-            load(q, t).start()
+    for t in range(tiles):
+        load(0, t).start()
     slot_lists = (h_slot, p_slot)
     own_rows, n_local = blocks.shape[1:3]
     lane_part = lax.broadcasted_iota(jnp.int32, (8, depth), 1) // b
@@ -129,9 +128,8 @@
             for e in range(cap):
                 row = jnp.where(lane == q * cap + e, fetch[0, e, o], row)
         message[o] = row
-    for t in range(tiles):
-        load(0, t).wait()
-    merge(0, theirs, 0, own_rows)
+    load(0, 0).wait()
+    merge(0, theirs, 0, cap)
     pl.semaphore_wait(barrier, n_rows + 1)
 
     def remote(src, dst, s, r, where):
@@ -149,12 +147,11 @@
     def rows_of(t):
         return pl.ds(t * tile, tile)
 
-    def scatter(q):
+    def scatter(q, t):
         source = merged.at[q, pl.ds(theirs, per_half)]
-        return [
-            start(remote(source.at[:, rows_of(t)], rs_buf.at[q, :, rows_of(t)], rs_s.at[q, t], rs_r.at[q, t], {"cols": sibling}))
-            for t in range(tiles)
-        ]
+        return start(
+            remote(source.at[:, rows_of(t)], rs_buf.at[q, :, rows_of(t)], rs_s.at[q, t], rs_r.at[q, t], {"cols": sibling})
+        )
 
     def add_cores(q, t, arriving):
         arriving.wait_recv()
@@ -192,7 +189,13 @@
         start(remote(message.at[right(k)], lists.at[me], list_s.at[k], list_r.at[k], {"rows": right(k)}))
         for k in range(1, n_rows)
     ]
-    h_scatter = scatter(0)
+    h_scatter = [scatter(0, 0)]
+    for t in range(1, tiles):
+        load(0, t).wait()
+        merge(0, theirs, t * cap, (t + 1) * cap)
+        h_scatter.append(scatter(0, t))
+    for t in range(tiles):
+        load(1, t).start()
     h_cross, p_cross = [], []
     for t in range(tiles):
         merge(0, mine, t * cap, (t + 1) * cap)
@@ -234,7 +237,7 @@
     for t in range(tiles):
         load(1, t).wait()
     merge(1, theirs, 0, own_rows)
-    p_scatter = scatter(1)
+    p_scatter = [scatter(1, t) for t in range(tiles)]
     merge(1, mine, 0, own_rows)
     for t in range(tiles):
         add_cores(1, t, p_scatter[t])
@@ -310,7 +313,7 @@
     vmem, smem = pl.BlockSpec(memory_space=pltpu.VMEM), pl.BlockSpec(memory_space=pltpu.SMEM)
     return pl.pallas_call(
         functools.partial(product_kernel, n_rows, n_cols, cap, b),
-        out_shape=jax.ShapeDtypeStruct((rows_all, columns), f32),
+        out_shape=pltpu.VMEM((rows_all, columns), f32),
         in_specs=[smem] * 4 + [pl.BlockSpec(memory_space=pltpu.HBM)] * 2 + [vmem],
         out_specs=vmem,
         scratch_shapes=[

time: 63.4 us -> 61.5 us (0.970)
  Pallas kernels: 61.1 us -> 59.9 us
  local copies, waits for them, and re-layouts: 1.87 us -> 0.8 us
    pallas_call x1, Pallas kernels: 61.1 us -> 59.9 us  [merged_body(): pl.pallas_call(functools.partial(product_kernel, n_rows, n_cols, cap, b),...]
    unnamed x1, local copies, waits for them, and re-layouts: 1.87 us -> 0.8 us
where the time goes in v4:
time: 61.5 us; the launch traced here: 60.7 us
  Pallas kernels  59.9 us (97%)
  local copies, waits for them, and re-layouts  0.8 us (1%)
    pallas_call x1, Pallas kernels, merged_body(): pl.pallas_call(functools.partial(product_kernel, n_rows, n_cols, cap, b),...  59.9 us

profile of v4, /device:TPU:0, one launch (start us, length us, event | category | flops | bytes accessed | tf_op | source)
XLA Modules:
  0.0 60.7 jit_solution(17696647942588642962)
XLA Ops:
  0.0 59.9 %product.1 = f32[512,256]{1,0:T(8,128)S(1)} custom-call(s32[8,48]{1,0:T(8,128)} %h_slot.1, s32[8,48]{1,0:T(8,128)} %p_slot.1, s32[1,2,8]{2,1,0:T(2,128)} %bitcast.4, s32[1,2,8]{2,1,0:T(2,128)} %bitcast.5, f32[8,12,64,64]{3,2,1,0:T(8,128)} %h_blocks.1, f32[8,12,64,64]{3,2,1,0:T(8,128)} %p_blocks.1, f32[8,64,256]{2,1,0:T(8,128)} %bitcast.3), custom_call_target="tpu_custom_call" | custom-call | tf_op jit(solution)/shard_map/product/pallas_call | solution.py:314
  59.9 0.8 %copy.9 = f32[512,256]{1,0:T(8,128)} copy(f32[512,256]{1,0:T(8,128)S(1)} %product.1) | data formatting | bytes 1048576
